TPU v7x, 32 devices: a whole 2x2x4 slice. The times are simulated.
32 devices in a mesh: row: 8 (over y, x, core), col: 4 (over z).
Axes of the slice: x: 2, y: 2, z: 4, core: 2. Of those that a mesh axis runs over, the one named last changes fastest.
Arguments:
- halves: bfloat16 [24, 800, 800], P(None, 'row', 'col'), may hold values from -6 to 6
- first_factor: bfloat16 [4000, 800], P('col'), may hold values from -0.21875 to 0.21875
- second_factor: bfloat16 [4000, 800], P('col'), may hold values from -0.09375 to 0.09375
- weights: bfloat16 [4000, 24], P('col'), may hold values from 0.25 to 4
Outputs:
- cycle: bfloat16 [24, 800, 800], P('col', 'row')
All inputs are finite; a program needn't handle non-finite values.
Results may differ from a plain program's by a relative error of at most 0.0095.
Values may be sent and summed in bfloat16 or wider, within the bound.
A program may use at most 64 MiB of HBM per device.

v0:
```python
import jax
import jax.numpy as jnp
from jax import lax
from jax.sharding import PartitionSpec as P


def body(halves, first_factor, second_factor, weights):
    regrouped = lax.all_to_all(halves, "col", split_axis=0, concat_axis=2, tiled=True)
    mirrored = lax.all_to_all(regrouped, "row", split_axis=2, concat_axis=1, tiled=True)
    amplitude = (
        regrouped.astype(jnp.float32) - jnp.swapaxes(mirrored, 1, 2).astype(jnp.float32)
    ).astype(jnp.bfloat16)
    gathered = lax.all_gather(amplitude, "col", axis=0, tiled=True)
    scaled = jnp.einsum("iab,qb->iaq", gathered, first_factor, preferred_element_type=jnp.float32)
    scaled = (scaled * jnp.transpose(weights).astype(jnp.float32)[:, None, :]).astype(jnp.bfloat16)
    return lax.psum_scatter(
        jnp.einsum("iaq,qc->iac", scaled, second_factor, preferred_element_type=jnp.float32).astype(
            jnp.bfloat16
        ),
        "col",
        scatter_dimension=0,
        tiled=True,
    )


def solution(mesh):
    placed = (P(None, "row", "col"), P("col", None), P("col", None), P("col", None))
    return jax.shard_map(
        body, mesh=mesh, in_specs=placed, out_specs=P("col", "row", None), check_vma=False
    )
```

profile of v0, /device:TPU:1, one launch (start us, length us, event | category | flops | bytes accessed | tf_op | source)
XLA Modules:
  0.0 273.2 jit_solution(1275359598515913316)
XLA Ops:
  6.5 0.0 copy-start
  6.5 0.0 all-gather.2.cloned.1.call-start
  6.5 2.2 copy.21
  8.8 34.2 %all_to_all.27 = bf16[24,100,200]{1,2,0:T(8,128)(2,1)S(1)} all-to-all(bf16[24,100,200]{1,2,0:T(8,128)(2,1)S(1)} %copy.21), channel_id=1, replica_groups=mesh['row'=8,'col'=4] {'col'}, dimensions={0} | all-to-all | bytes 1920000 | tf_op jit(solution)/shard_map/all_to_all | solution.py:8
  43.0 0.1 copy.22
  43.1 0.5 copy.23
  43.7 26.1 %all_to_all.28 = bf16[6,100,800]{1,0,2:T(8,128)(2,1)} all-to-all(bf16[6,100,800]{1,0,2:T(8,128)(2,1)S(1)} %copy.23), channel_id=1, replica_groups=mesh['row'=8,'col'=4] {'row'}, dimensions={2} | all-to-all | bytes 1920000 | tf_op jit(solution)/shard_map/all_to_all | solution.py:9
  69.7 3.7 %copy.24 = bf16[6,100,800]{2,1,0:T(8,128)(2,1)} copy(bf16[6,100,800]{1,0,2:T(8,128)(2,1)} %all_to_all.28) | data formatting | bytes 1920000 | tf_op jit(solution)/shard_map/all_to_all | solution.py:9
  73.4 3.4 %reshape.6 = f32[6,100,8,100]{3,2,1,0:T(8,128)} reshape(bf16[6,100,800]{2,1,0:T(8,128)(2,1)} %copy.24) | data formatting | bytes 2880000 | tf_op jit(solution)/shard_map/convert_element_type | solution.py:11
  76.9 3.6 %copy.28 = f32[6,8,100,100]{3,2,1,0:T(8,128)} copy(f32[6,8,100,100]{3,1,2,0:T(8,128)} %bitcast.21) | data formatting | bytes 3840000 | tf_op jit(solution)/shard_map/convert_element_type | solution.py:11
  80.5 3.2 %reshape.9 = f32[6,800,100]{2,1,0:T(8,128)} reshape(f32[6,8,100,100]{3,2,1,0:T(8,128)} %copy.28) | data formatting | bytes 3840000 | tf_op jit(solution)/shard_map/convert_element_type | solution.py:11
  83.7 3.0 %fusion.3 = bf16[6,100,800]{1,2,0:T(8,128)(2,1)} fusion(f32[6,800,100]{2,1,0:T(8,128)} %reshape.9, bf16[6,100,4,200]{1,3,2,0:T(8,128)(2,1)S(1)} %copy.22), kind=kLoop, calls=%fused_computation.5 | loop fusion | flops 1440000 | bytes 3840000 | tf_op jit(solution)/shard_map/convert_element_type | solution.py:12
  86.7 0.0 copy-start.1
  86.7 0.0 copy-start.2
  86.7 2.6 copy.27
  89.3 0.0 all-gather.2.cloned.1.call-update
  89.4 0.0 reduce-scatter.2.cloned.1.call-start
  89.4 0.0 copy-done.1
  89.4 82.8 %all-gather.2.cloned.1.call-done = bf16[24,100,800]{2,1,0:T(8,128)(2,1)} async-done(((bf16[6,100,800]{2,1,0:T(8,128)(2,1)}), bf16[24,100,800]{2,1,0:T(8,128)(2,1)}) %all-gather.2.cloned.1.call-update) | async-done | bytes 3840016 | tf_op jit(solution)/shard_map/all_gather | solution.py:13
  172.2 0.0 copy-done
  172.2 0.0 copy-done.2
  172.2 14.0 %fusion.2 = bf16[24,100,800]{2,1,0:T(8,128)(2,1)} fusion(f32[24,1000]{1,0:T(8,128)S(1)} %convert_bitcast_fusion, bf16[24,100,800]{2,1,0:T(8,128)(2,1)} %all-gather.2.cloned.1.call-done, bf16[1000,800]{0,1:T(8,128)(2,1)S(1)} %copy-done, bf16[1000,800]{0,1:T(8,128)(2,1)S(1)} %copy-done.2), kind=kOutput, calls=%fused_computation.3 | convolution fusion | flops 7686720000 | bytes 10976000 | tf_op jit(solution)/shard_map/iaq,qc->iac/dot_general | solution.py:17
  186.3 0.0 reduce-scatter.2.cloned.1.call-update
  186.3 80.1 %reduce-scatter.2.cloned.1.call-done = bf16[6,100,800]{2,1,0:T(8,128)(2,1)} async-done(((bf16[24,100,800]{2,1,0:T(8,128)(2,1)}), bf16[6,100,800]{2,1,0:T(8,128)(2,1)}) %reduce-scatter.2.cloned.1.call-update) | async-done | bytes 960016 | tf_op jit(solution)/shard_map/reduce_scatter | solution.py:16
  (1 shorter events, 0.0 us)
Async XLA Ops:
  6.5 165.7 %copy-start = (bf16[1000,800]{0,1:T(8,128)(2,1)S(1)}, bf16[1000,800]{0,1:T(8,128)(2,1)}, u32[]{:S(2)}) copy-start(bf16[1000,800]{0,1:T(8,128)(2,1)} %param.6) | copy-start | bytes 4800004
  6.5 165.7 %all-gather.2.cloned.1.call-start = ((), (), s32[]{:S(2)}) async-start(), calls=%async_computation.3 | async-start | bytes 5591040 | tf_op jit(solution)/shard_map/all_gather | solution.py:13
  86.7 2.7 copy-start.1
  86.7 85.6 %copy-start.2 = (bf16[1000,800]{0,1:T(8,128)(2,1)S(1)}, bf16[1000,800]{0,1:T(8,128)(2,1)}, u32[]{:S(2)}) copy-start(bf16[1000,800]{0,1:T(8,128)(2,1)} %param.5) | copy-start | bytes 4800004
  89.4 177.0 %reduce-scatter.2.cloned.1.call-start = ((), (), s32[]{:S(2)}) async-start(), calls=%async_computation.4 | async-start | bytes 5591040 | tf_op jit(solution)/shard_map/reduce_scatter | solution.py:16
Sparse Core Ops, SparseCore 0:
  89.5 82.7 all-gather.1
  186.4 79.9 reduce-scatter.1
where the time goes:
time: 274 us; the launch traced here: 273 us
  waiting for transfers between devices  163 us (59%)
  blocking collectives  60.3 us (22%)
  local copies, waits for them, and re-layouts  19.5 us (7%)
  matrix products  14 us (5%)
  between operations  13.4 us (5%)
  other arithmetic  2.98 us (1%)
    all_gather x1, waiting for transfers between devices, body(): gathered = lax.all_gather(amplitude, 'col', axis=0, tiled=True)  82.8 us
    reduce_scatter x1, waiting for transfers between devices, body(): lax.psum_scatter(jnp.einsum('iaq,qc->iac', scaled, second_factor, preferr...  80.1 us
    all_to_all x1, blocking collectives, body(): lax.all_to_all(halves, 'col', split_axis=0, concat_axis=2, tiled=True)  34.2 us
    all_to_all x1, blocking collectives, body(): lax.all_to_all(regrouped, 'row', split_axis=2, concat_axis=1, tiled=True)  26.1 us
    dot_general x1, matrix products, body(): jnp.einsum('iaq,qc->iac', scaled, second_factor, preferred_element_type=j...  14 us
    convert_element_type x3, local copies, waits for them, and re-layouts, body(): jnp.swapaxes(mirrored, 1, 2).astype(jnp.float32)  10.3 us
  transfers between devices with their start and end apart: 2, of which 2 were waited for; matrix products, arithmetic and copies ran while one was open for 0% of the time, Pallas kernels for 0%

commit v1 on v0

v1 whole, which is shorter than its diff:
```python
import jax
import jax.numpy as jnp
from jax import lax
from jax.sharding import PartitionSpec as P


def spread(block, rows):
    piece = -(-block.shape[0] // rows)
    pad = piece * rows - block.shape[0]
    if pad:
        block = jnp.pad(block, ((0, pad), (0, 0)))
    mine = lax.dynamic_slice_in_dim(block, lax.axis_index("row") * piece, piece, 0)
    everywhere = lax.all_gather(mine, "col", axis=0, tiled=False)
    return lax.all_gather(everywhere, "row", axis=0, tiled=False)


def body(rows, halves, first_factor, second_factor, weights):
    count = halves.shape[0] // lax.axis_size("col")
    first = spread(first_factor, rows)
    second = spread(second_factor, rows)
    scale = spread(weights, rows)
    first = first.reshape(-1, first.shape[-1])
    second = second.reshape(-1, second.shape[-1])
    scale = scale.reshape(-1, scale.shape[-1])
    scale = lax.dynamic_slice_in_dim(scale, lax.axis_index("col") * count, count, 1)
    regrouped = lax.all_to_all(halves, "col", split_axis=0, concat_axis=2, tiled=True)
    mirrored = lax.all_to_all(regrouped, "row", split_axis=2, concat_axis=1, tiled=True)
    amplitude = (
        regrouped.astype(jnp.float32) - jnp.swapaxes(mirrored, 1, 2).astype(jnp.float32)
    ).astype(jnp.bfloat16)
    scaled = jnp.einsum("iab,qb->iaq", amplitude, first, preferred_element_type=jnp.float32)
    scaled = (scaled * jnp.transpose(scale).astype(jnp.float32)[:, None, :]).astype(jnp.bfloat16)
    return jnp.einsum("iaq,qc->iac", scaled, second, preferred_element_type=jnp.float32).astype(
        jnp.bfloat16
    )


def solution(mesh):
    placed = (P(None, "row", "col"), P("col", None), P("col", None), P("col", None))
    rows = mesh.shape["row"]

    def run(*arrays):
        return body(rows, *arrays)

    return jax.shard_map(
        run, mesh=mesh, in_specs=placed, out_specs=P("col", "row", None), check_vma=False
    )
```

time: 274 us -> 205 us (0.75)
  waiting for transfers between devices: 163 us -> 0.04 us
  local copies, waits for them, and re-layouts: 19.5 us -> 66.9 us
  blocking collectives: 60.3 us -> 97.7 us
  starting transfers between devices: 0.04 us -> 7.17 us
  matrix products: 14 us -> 17.2 us
    all_gather x1 -> x2, waiting for transfers between devices: 82.8 us -> 0.01 us  [spread(): return lax.all_gather(everywhere, 'row', axis=0, tiled=False)]
    reduce_scatter x1 -> x0, waiting for transfers between devices: 80.1 us -> none  [body(): lax.psum_scatter(jnp.einsum('iaq,qc->iac', scaled, second_factor, preferr...]
    all_gather x0 -> x4, blocking collectives: none -> 67.9 us  [the longest x3 45.7 us: spread(): everywhere = lax.all_gather(mine, 'col', axis=0, tiled=False)]
    reshape x0 -> x3, local copies, waits for them, and re-layouts: none -> 29.3 us  [the longest x1 14.2 us: body(): first = first.reshape(-1, first.shape[-1])]
    all_to_all x1 -> x0, blocking collectives: 26.1 us -> none  [body(): lax.all_to_all(regrouped, 'row', split_axis=2, concat_axis=1, tiled=True)]
    all_gather x0 -> x3, local copies, waits for them, and re-layouts: none -> 16.3 us  [spread(): return lax.all_gather(everywhere, 'row', axis=0, tiled=False)]
    all_to_all x0 -> x1, starting transfers between devices: none -> 7.13 us  [body(): lax.all_to_all(regrouped, 'row', split_axis=2, concat_axis=1, tiled=True)]
    all_to_all x1, blocking collectives: 34.2 us -> 29.8 us  [body(): lax.all_to_all(halves, 'col', split_axis=0, concat_axis=2, tiled=True)]
  transfers between devices with their start and end apart: 2 -> 3, of which waited for: 2 -> 0; matrix products, arithmetic and copies ran while one was open for 0% -> 21% of each run, Pallas kernels for 0% -> 0%
where the time goes in v1:
time: 205 us; the launch traced here: 203 us
  blocking collectives  97.7 us (48%)
  local copies, waits for them, and re-layouts  66.9 us (33%)
  matrix products  17.2 us (8%)
  between operations  13.5 us (7%)
  starting transfers between devices  7.17 us (3%)
    all_gather x3, blocking collectives, spread(): everywhere = lax.all_gather(mine, 'col', axis=0, tiled=False)  45.7 us
    all_to_all x1, blocking collectives, body(): lax.all_to_all(halves, 'col', split_axis=0, concat_axis=2, tiled=True)  29.8 us
    all_gather x1, blocking collectives, spread(): return lax.all_gather(everywhere, 'row', axis=0, tiled=False)  22.2 us
    dot_general x1, matrix products, body(): jnp.einsum('iaq,qc->iac', scaled, second, preferred_element_type=jnp.floa...  17.2 us
    all_gather x3, local copies, waits for them, and re-layouts, spread(): return lax.all_gather(everywhere, 'row', axis=0, tiled=False)  16.3 us
    reshape x1, local copies, waits for them, and re-layouts, body(): first = first.reshape(-1, first.shape[-1])  14.2 us
    reshape x1, local copies, waits for them, and re-layouts, body(): second = second.reshape(-1, second.shape[-1])  14.1 us
    convert_element_type x3, local copies, waits for them, and re-layouts, body(): jnp.swapaxes(mirrored, 1, 2).astype(jnp.float32)  10.3 us
  transfers between devices with their start and end apart: 3, of which 0 were waited for; matrix products, arithmetic and copies ran while one was open for 21% of the time, Pallas kernels for 0%

profile of v1, /device:TPU:1, one launch (start us, length us, event | category | flops | bytes accessed | tf_op | source)
XLA Modules:
  0.0 203.4 jit_solution(6007250325783554869)
XLA Ops:
  6.5 1.4 copy-done
  8.0 0.1 dynamic-slice_bitcast_fusion
  8.1 18.8 %all-gather.8 = bf16[4,125,800]{1,2,0:T(8,128)(2,1)} all-gather(bf16[1,125,800]{1,2,0:T(8,128)(2,1)S(1)} %dynamic-slice_bitcast_fusion), channel_id=6, replica_groups=mesh['row'=8,'col'=4] {'col'}, dimensions={0}, use_global_device_ids=true | all-gather | bytes 1000000 | tf_op jit(solution)/shard_map/all_gather | solution.py:13
  27.0 1.1 dynamic-slice_bitcast_fusion.1
  28.1 16.7 %all-gather.6 = bf16[4,125,800]{1,2,0:T(8,128)(2,1)} all-gather(bf16[1,125,800]{1,2,0:T(8,128)(2,1)S(1)} %dynamic-slice_bitcast_fusion.1), channel_id=2, replica_groups=mesh['row'=8,'col'=4] {'col'}, dimensions={0}, use_global_device_ids=true | all-gather | bytes 1000000 | tf_op jit(solution)/shard_map/all_gather | solution.py:13
  44.9 2.1 %copy.29 = bf16[24,100,200]{1,2,0:T(8,128)(2,1)S(1)} copy(bf16[24,100,200]{2,0,1:T(8,128)(2,1)} %param.4) | data formatting | bytes 1920000 | tf_op args[0]
  47.0 29.8 %all_to_all.27 = bf16[24,100,200]{1,2,0:T(8,128)(2,1)S(1)} all-to-all(bf16[24,100,200]{1,2,0:T(8,128)(2,1)S(1)} %copy.29), channel_id=1, replica_groups=mesh['row'=8,'col'=4] {'col'}, dimensions={0} | all-to-all | bytes 1920000 | tf_op jit(solution)/shard_map/all_to_all | solution.py:26
  76.9 1.1 copy-done.1
  77.9 1.7 copy.31
  79.6 7.1 %all-to-all-start.1 = ((bf16[6,100,800]{1,0,2:T(8,128)(2,1)}), bf16[6,100,800]{1,0,2:T(8,128)(2,1)S(1)}, u32[]{:S(2)}, u32[]{:S(2)}) async-start(bf16[6,100,800]{1,0,2:T(8,128)(2,1)} %copy.31), calls=%async_computation.1 | async-start | bytes 3276800 | tf_op jit(solution)/shard_map/all_to_all | solution.py:27
  86.8 0.8 dynamic-slice_bitcast_fusion.2
  87.5 10.2 %all-gather.7 = bf16[4,125,24]{1,2,0:T(8,128)(2,1)S(1)} all-gather(bf16[1,125,24]{1,2,0:T(8,128)(2,1)S(1)} %dynamic-slice_bitcast_fusion.2), channel_id=4, replica_groups=mesh['row'=8,'col'=4] {'col'}, dimensions={0}, use_global_device_ids=true | all-gather | bytes 30000 | tf_op jit(solution)/shard_map/all_gather | solution.py:13
  97.8 22.2 %all-gather.3 = bf16[32,125,24]{1,2,0:T(8,128)(2,1)S(1)} all-gather(bf16[4,125,24]{1,2,0:T(8,128)(2,1)S(1)} %all-gather.7), channel_id=5, replica_groups=mesh['row'=8,'col'=4] {'row'}, dimensions={0}, use_global_device_ids=true | all-gather | bytes 216000 | tf_op jit(solution)/shard_map/all_gather | solution.py:14
  120.0 1.0 reshape.15
  121.0 0.9 convert_bitcast_fusion
  121.9 2.6 %copy.32 = bf16[6,100,800]{2,1,0:T(8,128)(2,1)} copy(bf16[6,100,800]{1,0,2:T(8,128)(2,1)S(1)} %all-to-all-done.1) | data formatting | bytes 1920000 | tf_op jit(solution)/shard_map/all_to_all | solution.py:27
  124.5 3.5 %reshape.18 = f32[6,100,8,100]{3,2,1,0:T(8,128)} reshape(bf16[6,100,800]{2,1,0:T(8,128)(2,1)} %copy.32) | data formatting | bytes 2880000 | tf_op jit(solution)/shard_map/convert_element_type | solution.py:29
  128.0 3.6 %copy.40 = f32[6,8,100,100]{3,2,1,0:T(8,128)} copy(f32[6,8,100,100]{3,1,2,0:T(8,128)} %bitcast.28) | data formatting | bytes 3840000 | tf_op jit(solution)/shard_map/convert_element_type | solution.py:29
  131.6 3.2 %reshape.39 = f32[6,800,100]{2,1,0:T(8,128)} reshape(f32[6,8,100,100]{3,2,1,0:T(8,128)} %copy.40) | data formatting | bytes 3840000 | tf_op jit(solution)/shard_map/convert_element_type | solution.py:29
  134.9 8.2 %copy.38 = bf16[32,125,800]{1,0,2:T(8,128)(2,1)} copy(bf16[32,125,800]{1,2,0:T(8,128)(2,1)} %all-gather.14.cloned.1.call-done) | data formatting | bytes 12800000 | tf_op jit(solution)/shard_map/all_gather | solution.py:14
  143.0 14.1 %reshape.38 = bf16[4000,800,1]{0,1,2:T(8,128)(2,1)} reshape(bf16[32,125,800]{1,0,2:T(8,128)(2,1)} %copy.38) | data formatting | bytes 12800000 | tf_op jit(solution)/shard_map/reshape | solution.py:23
  157.1 8.1 %copy.35 = bf16[32,125,800]{1,0,2:T(8,128)(2,1)} copy(bf16[32,125,800]{1,2,0:T(8,128)(2,1)} %all-gather.12.cloned.1.call-done) | data formatting | bytes 12800000 | tf_op jit(solution)/shard_map/all_gather | solution.py:14
  165.2 14.2 %reshape.37 = bf16[4000,800,1]{0,1,2:T(8,128)(2,1)} reshape(bf16[32,125,800]{1,0,2:T(8,128)(2,1)} %copy.35) | data formatting | bytes 12800000 | tf_op jit(solution)/shard_map/reshape | solution.py:22
  179.4 17.2 %convolution_convert_fusion = bf16[6,100,800]{2,1,0:T(8,128)(2,1)} fusion(bf16[4000,800,1]{0,1,2:T(8,128)(2,1)} %reshape.38, bf16[4000,800,1]{0,1,2:T(8,128)(2,1)} %reshape.37, f32[6,4000]{1,0:T(8,128)S(1)} %convert_bitcast_fusion, f32[6,800,100]{2,1,0:T(8,128)} %reshape.39, bf16[6,100,800]{1,2,0:T(8,128)(2,1)S(1)} %bitcast.30), kind=kOutput, calls=%fused_computation.3 | convolution fusion | flops 7686720512 | bytes 16736000 | tf_op jit(solution)/shard_map/iaq,qc->iac/dot_general | solution.py:33
  (13 shorter events, 0.2 us)
Async XLA Ops:
  6.5 1.4 copy-start
  6.5 128.3 %all-gather.14.cloned.1.call-start = ((), (), s32[]{:S(2)}) async-start(), calls=%async_computation.3 | async-start | bytes 7372800 | tf_op jit(solution)/shard_map/all_gather | solution.py:14
  26.9 130.2 %all-gather.12.cloned.1.call-start = ((), (), s32[]{:S(2)}) async-start(), calls=%async_computation.2 | async-start | bytes 7372800 | tf_op jit(solution)/shard_map/all_gather | solution.py:14
  76.9 1.1 copy-start.1
  79.6 42.3 %all-to-all-start.1 = ((bf16[6,100,800]{1,0,2:T(8,128)(2,1)}), bf16[6,100,800]{1,0,2:T(8,128)(2,1)S(1)}, u32[]{:S(2)}, u32[]{:S(2)}) async-start(bf16[6,100,800]{1,0,2:T(8,128)(2,1)} %copy.31), calls=%async_computation.1 | async-start | bytes 3276800 | tf_op jit(solution)/shard_map/all_to_all | solution.py:27
  165.2 14.2 %copy-start.2 = (bf16[6,100,4,200]{1,3,2,0:T(8,128)(2,1)S(1)}, bf16[6,100,4,200]{1,3,2,0:T(8,128)(2,1)}, u32[]{:S(2)}) copy-start(bf16[6,100,4,200]{1,3,2,0:T(8,128)(2,1)} %copy-done.1) | copy-start | bytes 2880004
Sparse Core Ops, SparseCore 0:
  27.1 49.3 all-gather.13
  78.3 63.1 all-gather.11

commit v2 on v1

--- a/solution.py
+++ b/solution.py
@@ -1,6 +1,10 @@
+import functools
+
 import jax
 import jax.numpy as jnp
 from jax import lax
+from jax.experimental import pallas as pl
+from jax.experimental.pallas import tpu as pltpu
 from jax.sharding import PartitionSpec as P
 
 
@@ -35,11 +39,201 @@
     )
 
 
+def up(value, unit):
+    return -(-value // unit) * unit
+
+
+def kernel(R, Z, n, wide, L, fin, hin, out, F, X, Y, A, acc, ws, rs, rr,
+           fz_s, fz_r, fp_s, fp_r, h_s, h_r, y_s, y_r, a_s, a_r, r_s, r_r, loc):
+    f32, bf16 = jnp.float32, jnp.bfloat16
+    S, C = R // Z, R // 2
+    count, tall, lanes = X.shape[1:]
+    K = A.shape[2]
+    r, z = lax.axis_index("row"), lax.axis_index("col")
+    p, core = r // 2, lax.rem(r, 2)
+    mate = r + 1 - 2 * core
+
+    def send(src, dst, ss, sr, row, col):
+        return pltpu.make_async_remote_copy(
+            src_ref=src, dst_ref=dst, send_sem=ss, recv_sem=sr,
+            device_id={"row": row, "col": col}, device_id_type=pl.DeviceIdType.MESH)
+
+    barrier = pltpu.get_barrier_semaphore()
+    for d in range(1, R):
+        pl.semaphore_signal(barrier, inc=1, device_id={"row": lax.rem(r + d, R), "col": z},
+                            device_id_type=pl.DeviceIdType.MESH)
+    for d in range(1, Z):
+        pl.semaphore_signal(barrier, inc=1, device_id={"row": r, "col": lax.rem(z + d, Z)},
+                            device_id_type=pl.DeviceIdType.MESH)
+    pl.semaphore_wait(barrier, R + Z - 2)
+
+    sent = []
+    own = pltpu.make_async_copy(hin.at[pl.ds(z * S, S)], X.at[pl.ds(z * S, S)], loc)
+    piece = pl.ds(pl.multiple_of(p * wide, 128), wide)
+    hs, fs = [], []
+    for d in range(1, Z):
+        to = lax.rem(z + d, Z)
+        hs.append(send(hin.at[pl.ds(to * S, S)], X.at[pl.ds(z * S, S)], h_s.at[d - 1], h_r.at[d - 1], r, to))
+        fs.append(send(fin.at[:, piece], F.at[z, :, piece], fz_s.at[d - 1], fz_r.at[d - 1], r, to))
+    for c in hs + fs:
+        c.start()
+    own.start()
+    sent += hs + fs
+
+    for c in hs:
+        c.wait_recv()
+    own.wait()
+    ys = []
+    for d in range(1, R):
+        to = lax.rem(r + d, R)
+        ys.append(send(X.at[to], Y.at[r], y_s.at[d - 1], y_r.at[d - 1], to, z))
+        ys[-1].start()
+    mine = pltpu.make_async_copy(X.at[r], Y.at[r], loc)
+    mine.start()
+    sent += ys
+    fps = {}
+    for d in range(1, Z):
+        fs[d - 1].wait_recv()
+        src = lax.rem(z + Z - d, Z)
+        for e in range(1, C):
+            to = lax.rem(p + e, C) * 2 + core
+            c = send(F.at[src, :, piece], F.at[src, :, piece], fp_s.at[d - 1, e - 1], fp_r.at[d - 1, e - 1], to, z)
+            c.start()
+            fps[d, e] = c
+            sent.append(c)
+    for c in ys:
+        c.wait_recv()
+    mine.wait()
+
+    @pl.loop(0, count)
+    def _(i):
+        tiles = [jnp.zeros((tall, lanes), f32) for _ in range(K // 128)]
+        for j in range(R):
+            y = jnp.concatenate([Y[j, i].astype(f32), jnp.zeros((lanes - tall, lanes), f32)], axis=0)
+            v = X[j, i].astype(f32) - jnp.transpose(y)[:tall]
+            q, rem = divmod(j * tall, 128)
+            if rem + tall <= 128:
+                tiles[q] += pltpu.roll(v, rem, 1) if rem else v
+            else:
+                w = pltpu.roll(v, rem, 1)
+                at = lax.broadcasted_iota(jnp.int32, (tall, lanes), 1)
+                tiles[q] += jnp.where(at >= rem, w, 0.0)
+                tiles[q + 1] += jnp.where(at < rem, w, 0.0)
+        start = pl.multiple_of(i * tall, 16)
+        for q in range(K // 128):
+            A[0, pl.ds(start, tall), pl.ds(q * 128, 128)] = tiles[q].astype(bf16)
+
+    swap = send(A.at[0], A.at[1], a_s, a_r, mate, z)
+    swap.start()
+    sent.append(swap)
+
+    half = count // 2 if count % 2 == 0 else count
+    top = K + n
+
+    def compute(block, slot, first):
+        @pl.loop(0, count // half)
+        def _(c):
+            rows = pl.ds(pl.multiple_of(c * half * tall, 16), half * tall)
+            t = jnp.dot(A[slot, rows, :], block[0:K, :], preferred_element_type=f32)
+            t = jnp.concatenate(
+                [t[g * tall:(g + 1) * tall] * ws[pl.ds(c * half + g, 1), :] for g in range(half)], axis=0
+            ).astype(bf16)
+            o = lax.dot_general(t, block[K:top, :], (((1,), (1,)), ((), ())), preferred_element_type=f32)
+            if first:
+                acc[slot, rows, :] = o
+            else:
+                acc[slot, rows, :] += o
+
+    back = send(rs, rr, r_s, r_r, mate, z)
+    sent.append(back)
+    for d in range(Z):
+        if d:
+            for e in range(1, C):
+                fps[d, e].wait_recv()
+            block = F.at[lax.rem(z + Z - d, Z)]
+        else:
+            block = fin
+        shape = (ws.shape[0], L - top)
+        pick = lax.broadcasted_iota(jnp.int32, shape, 1) == lax.broadcasted_iota(jnp.int32, shape, 0) + z * count
+        ws[...] = jnp.dot(jnp.where(pick, 1.0, 0.0).astype(bf16), block[top:L, :], preferred_element_type=f32)
+        if d == 0:
+            compute(block, 0, True)
+            swap.wait_recv()
+            compute(block, 1, True)
+        else:
+            compute(block, 1, False)
+            if d == Z - 1:
+                rs[...] = acc[1].astype(bf16)
+                back.start()
+            compute(block, 0, False)
+    back.wait_recv()
+    for i in range(count):
+        rows = slice(i * tall, (i + 1) * tall)
+        out[i] = (acc[0, rows, :] + rr[rows, :].astype(f32)).astype(bf16)[: out.shape[1]]
+    for c in sent:
+        c.wait_send()
+
+
+def fused(R, Z, halves, first_factor, second_factor, weights):
+    bf16 = jnp.bfloat16
+    S, C = R // Z, R // 2
+    O, a, b = halves.shape
+    q, v = first_factor.shape
+    n = second_factor.shape[1]
+    count, step = O // Z, b // S
+    tall, lanes = up(a, 16), 128
+    K = up(R * tall, 128)
+    wide = up(-(-q // R), 128)
+    core = lax.rem(lax.axis_index("row"), 2)
+    one = first_factor.T.reshape(R, a, q)
+    one = jnp.pad(one, ((0, 0), (0, tall - a), (0, 0))).reshape(R * tall, q)
+    w = weights.T
+    L = up(K + n + O, 16)
+    full = jnp.concatenate([jnp.pad(one, ((0, K - R * tall), (0, 0))), second_factor.T, w], axis=0)
+    full = jnp.pad(full, ((0, L - K - n - O), (0, R * wide - q)))
+    fin = lax.dynamic_slice_in_dim(full, core * (C * wide), C * wide, 1)
+    hin = halves.reshape(Z, count, a, S, step).transpose(0, 3, 1, 2, 4).reshape(R, count, a, step)
+    hin = jnp.pad(hin, ((0, 0), (0, 0), (0, tall - a), (0, lanes - step)))
+    dma, vmem = pltpu.SemaphoreType.DMA, pltpu.VMEM
+    big = pl.BlockSpec(memory_space=pltpu.VMEM)
+    return pl.pallas_call(
+        functools.partial(kernel, R, Z, n, wide, L),
+        out_shape=jax.ShapeDtypeStruct((count, a, n), bf16),
+        in_specs=[big, big],
+        out_specs=big,
+        scratch_shapes=[
+            vmem((Z, L, C * wide), bf16),
+            vmem((R, count, tall, lanes), bf16),
+            vmem((R, count, tall, lanes), bf16),
+            vmem((2, count * tall, K), bf16),
+            vmem((2, count * tall, n), jnp.float32),
+            vmem((up(count, 16), C * wide), jnp.float32),
+            vmem((count * tall, n), bf16),
+            vmem((count * tall, n), bf16),
+            dma((Z - 1,)), dma((Z - 1,)),
+            dma((Z - 1, C - 1)), dma((Z - 1, C - 1)),
+            dma((Z - 1,)), dma((Z - 1,)),
+            dma((R - 1,)), dma((R - 1,)),
+            dma, dma, dma, dma, dma,
+        ],
+        compiler_params=pltpu.CompilerParams(
+            collective_id=0, has_side_effects=True, vmem_limit_bytes=56 * 1024 * 1024
+        ),
+    )(fin, hin)
+
+
+def fits(mesh):
+    R, Z = mesh.shape["row"], mesh.shape["col"]
+    return R % Z == 0 and R % 2 == 0 and R <= 8
+
+
 def solution(mesh):
     placed = (P(None, "row", "col"), P("col", None), P("col", None), P("col", None))
-    rows = mesh.shape["row"]
+    rows, cols = mesh.shape["row"], mesh.shape["col"]
 
     def run(*arrays):
+        if fits(mesh):
+            return fused(rows, cols, *arrays)
         return body(rows, *arrays)
 
     return jax.shard_map(

time: 205 us -> 145 us (0.71)
  the two profiles are of different devices: /device:TPU:1 before, /device:TPU:9 now
where the time goes in v2:
time: 145 us
  Pallas kernels  135 us (93%)
  local copies, waits for them, and re-layouts  7.73 us (5%)
  other arithmetic  2.1 us (1%)
    pallas_call x1, Pallas kernels, fused(): pl.pallas_call(functools.partial(kernel, R, Z, n, wide, L), out_shape=jax...  135 us
    unnamed x7, local copies, waits for them, and re-layouts  3.5 us

profile of v2, /device:TPU:9, one launch (start us, length us, event | category | flops | bytes accessed | tf_op | source)
XLA Modules:
  0.0 145.0 jit_solution(5944405010256602446)
XLA Ops:
  0.0 1.6 %reshape.12 = bf16[8,100,1000]{2,1,0:T(8,128)(2,1)S(1)} reshape(bf16[800,1000]{1,0:T(8,128)(2,1)} %bitcast.11) | data formatting | bytes 3200000 | tf_op jit(solution)/shard_map/reshape | solution.py:188
  1.6 0.0 copy-start
  1.6 0.0 copy-start.2
  1.6 0.3 pad.12
  1.9 1.2 copy-done
  3.1 0.0 copy-done.2
  3.1 0.0 copy-start.1
  3.1 2.1 %fusion.6.fin = bf16[1728,512]{1,0:T(8,128)(2,1)} fusion(s32[]{:T(128)S(6)} %select_n.3, bf16[896,1000]{1,0:T(8,128)(2,1)S(1)} %bitcast.9, bf16[800,1000]{1,0:T(8,128)(2,1)S(1)} %bitcast.12, bf16[24,1000]{1,0:T(8,128)(2,1)S(1)} %bitcast.13), kind=kLoop, calls=%fused_computation.11 | loop fusion | flops 14155776 | bytes 5210496 | tf_op jit(solution)/shard_map/concatenate | solution.py:192
  5.2 0.0 copy-done.1
  5.2 0.7 reshape.14
  5.8 0.3 copy.6
  6.2 1.4 pad.14.hin
  7.6 135.1 %shard_map.46 = bf16[6,100,800]{2,1,0:T(8,128)(2,1)} custom-call(bf16[1728,512]{1,0:T(8,128)(2,1)} %fusion.6.fin, bf16[8,6,112,128]{3,2,1,0:T(8,128)(2,1)} %pad.14.hin), custom_call_target="tpu_custom_call" | custom-call | tf_op jit(solution)/shard_map/pallas_call | solution.py:199
  142.6 2.3 %copy.8 = bf16[6,100,800]{2,1,0:T(8,128)(2,1)} copy(bf16[6,100,800]{2,1,0:T(8,128)(2,1)} %shard_map.46) | data formatting | bytes 1920000
Async XLA Ops:
  1.6 1.4 copy-start
  1.6 1.4 copy-start.2
  3.1 2.1 %copy-start.1 = (bf16[24,100,200]{2,0,1:T(8,128)(2,1)S(1)}, bf16[24,100,200]{2,0,1:T(8,128)(2,1)}, u32[]{:S(2)}) copy-start(bf16[24,100,200]{2,0,1:T(8,128)(2,1)} %param.4) | copy-start | bytes 2880004

commit v3 on v2

--- a/solution.py
+++ b/solution.py
@@ -44,10 +44,11 @@
 
 
 def kernel(R, Z, n, wide, L, fin, hin, out, F, X, Y, A, acc, ws, rs, rr,
-           fz_s, fz_r, fp_s, fp_r, h_s, h_r, y_s, y_r, a_s, a_r, r_s, r_r, loc):
+           fz_s, fz_r, fp_s, fp_r, fd_s, fd_r, h_s, h_r, y_s, y_r, a_s, a_r, r_s, r_r, loc):
     f32, bf16 = jnp.float32, jnp.bfloat16
     S, C = R // Z, R // 2
     count, tall, lanes = X.shape[1:]
+    size = out.shape[1]
     K = A.shape[2]
     r, z = lax.axis_index("row"), lax.axis_index("col")
     p, core = r // 2, lax.rem(r, 2)
@@ -69,17 +70,66 @@
 
     sent = []
     own = pltpu.make_async_copy(hin.at[pl.ds(z * S, S)], X.at[pl.ds(z * S, S)], loc)
-    piece = pl.ds(pl.multiple_of(p * wide, 128), wide)
-    hs, fs = [], []
+    px, py = p + 1 - 2 * lax.rem(p, 2), lax.rem(p + 2, C)
+
+    def lane(q):
+        return pl.ds(pl.multiple_of(q * wide, 128), wide)
+
+    def along(side, step, src, src_ref):
+        return send(src_ref, F.at[src, :, lane(p)], fz_s.at[side, step - 1], fz_r.at[side, step - 1],
+                    r, z + 1 - 2 * side)
+
+    firsts = [along(side, 1, z, fin.at[:, lane(p)]) for side in range(2)]
+    can = [z + 1 < Z, z > 0]
+    for side in range(2):
+        pl.when(can[side])(firsts[side].start)
+    hs = []
     for d in range(1, Z):
         to = lax.rem(z + d, Z)
         hs.append(send(hin.at[pl.ds(to * S, S)], X.at[pl.ds(z * S, S)], h_s.at[d - 1], h_r.at[d - 1], r, to))
-        fs.append(send(fin.at[:, piece], F.at[z, :, piece], fz_s.at[d - 1], fz_r.at[d - 1], r, to))
-    for c in hs + fs:
-        c.start()
+        hs[-1].start()
     own.start()
-    sent += hs + fs
-
+    sent += hs
+
+    near = jnp.minimum(z, Z - 1 - z)
+    longer = jnp.where(z > Z - 1 - z, 0, 1)
+    blocks = []
+    cut = L // 32 * 16
+    for k in range(1, Z):
+        paired = k <= 2 * near
+        step = jnp.where(paired, (k + 1) // 2, k - near)
+        side = jnp.where(paired, (k - 1) % 2, longer)
+        src = z + step * (2 * side - 1)
+        come = along(side, step, src, F.at[src, :, lane(p)])
+        go = along(side, step + 1, src, F.at[src, :, lane(p)])
+        on = jnp.where(side == 0, z + 1 < Z, z > 0)
+        mine = F.at[src, :, lane(p)]
+        plane = [send(mine, mine, fp_s.at[k - 1, g], fp_r.at[k - 1, g], to * 2 + core, z)
+                 for g, to in enumerate((px, py))]
+        high = F.at[src, pl.ds(0, cut), lane(px)]
+        low = F.at[src, pl.ds(cut, L - cut), lane(py)]
+        corner = [send(high, high, fd_s.at[k - 1, 0], fd_r.at[k - 1, 0], py * 2 + core, z),
+                  send(low, low, fd_s.at[k - 1, 1], fd_r.at[k - 1, 1], px * 2 + core, z)]
+        blocks.append((src, come, go, on, plane, corner))
+        sent += plane + corner
+
+    def arrive(k):
+        src, come, go, on, plane, corner = blocks[k - 1]
+        come.wait_recv()
+        pl.when(on)(go.start)
+        for c in plane:
+            c.start()
+
+    def turn(k):
+        plane, corner = blocks[k - 1][4:]
+        for c, f in zip(plane, corner):
+            c.wait_recv()
+            f.start()
+
+    arrive(1)
+    for k in range(2, Z - 1):
+        arrive(k)
+    turn(1)
     for c in hs:
         c.wait_recv()
     own.wait()
@@ -91,16 +141,10 @@
     mine = pltpu.make_async_copy(X.at[r], Y.at[r], loc)
     mine.start()
     sent += ys
-    fps = {}
-    for d in range(1, Z):
-        fs[d - 1].wait_recv()
-        src = lax.rem(z + Z - d, Z)
-        for e in range(1, C):
-            to = lax.rem(p + e, C) * 2 + core
-            c = send(F.at[src, :, piece], F.at[src, :, piece], fp_s.at[d - 1, e - 1], fp_r.at[d - 1, e - 1], to, z)
-            c.start()
-            fps[d, e] = c
-            sent.append(c)
+    for k in range(2, Z - 1):
+        turn(k)
+    if Z > 2:
+        arrive(Z - 1)
     for c in ys:
         c.wait_recv()
     mine.wait()
@@ -111,8 +155,8 @@
         for j in range(R):
             y = jnp.concatenate([Y[j, i].astype(f32), jnp.zeros((lanes - tall, lanes), f32)], axis=0)
             v = X[j, i].astype(f32) - jnp.transpose(y)[:tall]
-            q, rem = divmod(j * tall, 128)
-            if rem + tall <= 128:
+            q, rem = divmod(j * size, 128)
+            if rem + size <= 128:
                 tiles[q] += pltpu.roll(v, rem, 1) if rem else v
             else:
                 w = pltpu.roll(v, rem, 1)
@@ -128,7 +172,7 @@
     sent.append(swap)
 
     half = count // 2 if count % 2 == 0 else count
-    top = K + n
+    low, top = R * size, R * size + n
 
     def compute(block, slot, first):
         @pl.loop(0, count // half)
@@ -138,7 +182,7 @@
             t = jnp.concatenate(
                 [t[g * tall:(g + 1) * tall] * ws[pl.ds(c * half + g, 1), :] for g in range(half)], axis=0
             ).astype(bf16)
-            o = lax.dot_general(t, block[K:top, :], (((1,), (1,)), ((), ())), preferred_element_type=f32)
+            o = lax.dot_general(t, block[low:top, :], (((1,), (1,)), ((), ())), preferred_element_type=f32)
             if first:
                 acc[slot, rows, :] = o
             else:
@@ -146,23 +190,25 @@
 
     back = send(rs, rr, r_s, r_r, mate, z)
     sent.append(back)
-    for d in range(Z):
-        if d:
-            for e in range(1, C):
-                fps[d, e].wait_recv()
-            block = F.at[lax.rem(z + Z - d, Z)]
+    for k in range(Z):
+        if k:
+            for c in blocks[k - 1][5]:
+                c.wait_recv()
+            block = F.at[blocks[k - 1][0]]
         else:
             block = fin
         shape = (ws.shape[0], L - top)
         pick = lax.broadcasted_iota(jnp.int32, shape, 1) == lax.broadcasted_iota(jnp.int32, shape, 0) + z * count
         ws[...] = jnp.dot(jnp.where(pick, 1.0, 0.0).astype(bf16), block[top:L, :], preferred_element_type=f32)
-        if d == 0:
+        if k == 0:
             compute(block, 0, True)
             swap.wait_recv()
             compute(block, 1, True)
+            if Z > 2:
+                turn(Z - 1)
         else:
             compute(block, 1, False)
-            if d == Z - 1:
+            if k == Z - 1:
                 rs[...] = acc[1].astype(bf16)
                 back.start()
             compute(block, 0, False)
@@ -172,6 +218,10 @@
         out[i] = (acc[0, rows, :] + rr[rows, :].astype(f32)).astype(bf16)[: out.shape[1]]
     for c in sent:
         c.wait_send()
+    for side in range(2):
+        pl.when(can[side])(firsts[side].wait_send)
+    for block in blocks:
+        pl.when(block[3])(block[2].wait_send)
 
 
 def fused(R, Z, halves, first_factor, second_factor, weights):
@@ -182,15 +232,12 @@
     n = second_factor.shape[1]
     count, step = O // Z, b // S
     tall, lanes = up(a, 16), 128
-    K = up(R * tall, 128)
+    K = up(R * a, 128)
     wide = up(-(-q // R), 128)
     core = lax.rem(lax.axis_index("row"), 2)
-    one = first_factor.T.reshape(R, a, q)
-    one = jnp.pad(one, ((0, 0), (0, tall - a), (0, 0))).reshape(R * tall, q)
-    w = weights.T
-    L = up(K + n + O, 16)
-    full = jnp.concatenate([jnp.pad(one, ((0, K - R * tall), (0, 0))), second_factor.T, w], axis=0)
-    full = jnp.pad(full, ((0, L - K - n - O), (0, R * wide - q)))
+    L = up(R * a + n + O, 16)
+    full = jnp.concatenate([first_factor.T, second_factor.T, weights.T], axis=0)
+    full = jnp.pad(full, ((0, L - R * a - n - O), (0, R * wide - q)))
     fin = lax.dynamic_slice_in_dim(full, core * (C * wide), C * wide, 1)
     hin = halves.reshape(Z, count, a, S, step).transpose(0, 3, 1, 2, 4).reshape(R, count, a, step)
     hin = jnp.pad(hin, ((0, 0), (0, 0), (0, tall - a), (0, lanes - step)))
@@ -210,8 +257,9 @@
             vmem((up(count, 16), C * wide), jnp.float32),
             vmem((count * tall, n), bf16),
             vmem((count * tall, n), bf16),
-            dma((Z - 1,)), dma((Z - 1,)),
-            dma((Z - 1, C - 1)), dma((Z - 1, C - 1)),
+            dma((2, Z)), dma((2, Z)),
+            dma((Z - 1, 2)), dma((Z - 1, 2)),
+            dma((Z - 1, 2)), dma((Z - 1, 2)),
             dma((Z - 1,)), dma((Z - 1,)),
             dma((R - 1,)), dma((R - 1,)),
             dma, dma, dma, dma, dma,
@@ -224,7 +272,7 @@
 
 def fits(mesh):
     R, Z = mesh.shape["row"], mesh.shape["col"]
-    return R % Z == 0 and R % 2 == 0 and R <= 8
+    return R % Z == 0 and R == 8 and Z > 2
 
 
 def solution(mesh):

time: 145 us -> 115 us (0.79)
  the two profiles are of different devices: /device:TPU:9 before, /device:TPU:1 now
where the time goes in v3:
time: 115 us
  Pallas kernels  105 us (91%)
  local copies, waits for them, and re-layouts  8 us (7%)
  other arithmetic  2.01 us (2%)
    pallas_call x1, Pallas kernels, fused(): pl.pallas_call(functools.partial(kernel, R, Z, n, wide, L), out_shape=jax...  105 us
    reshape x2, local copies, waits for them, and re-layouts, fused(): halves.reshape(Z, count, a, S, step).transpose(0, 3, 1, 2, 4)  3.52 us
    unnamed x7, local copies, waits for them, and re-layouts  3.13 us

profile of v3, /device:TPU:1, one launch (start us, length us, event | category | flops | bytes accessed | tf_op | source)
XLA Modules:
  0.0 115.1 jit_solution(6021911109105607064)
XLA Ops:
  0.0 3.2 %reshape.6 = bf16[4,6,100,2,100]{4,3,1,0,2:T(2,128)(2,1)S(1)} reshape(bf16[24,100,200]{2,0,1:T(8,128)(2,1)} %param.4) | data formatting | bytes 1920000 | tf_op jit(solution)/shard_map/reshape | solution.py:242
  3.2 0.0 copy-start.1
  3.2 0.3 copy.5
  3.5 0.0 copy-start
  3.6 0.0 copy-start.2
  3.6 1.4 %pad.9.hin = bf16[8,6,112,128]{3,2,1,0:T(8,128)(2,1)} pad(bf16[8,6,100,100]{3,2,1,0:T(8,128)(2,1)S(1)} %bitcast.8, bf16[]{:T(256)} %constant.5.clone.1), padding=0_0x0_0x0_12x0_28 | pad | bytes 2336258 | tf_op jit(solution)/shard_map/jit(_pad)/pad | solution.py:243
  4.9 0.0 copy-done.1
  4.9 0.8 copy-done
  5.7 0.0 copy-done.2
  5.7 2.0 %fusion.6.fin = bf16[1632,512]{1,0:T(8,128)(2,1)} fusion(s32[]{:T(128)S(6)} %select_n.3, bf16[800,1000]{1,0:T(8,128)(2,1)S(1)} %bitcast.9, bf16[800,1000]{1,0:T(8,128)(2,1)S(1)} %bitcast.10, bf16[24,1000]{1,0:T(8,128)(2,1)S(1)} %bitcast.11), kind=kLoop, calls=%fused_computation.11 | loop fusion | flops 13369344 | bytes 4920192 | tf_op jit(solution)/shard_map/concatenate | solution.py:239
  7.7 105.0 %shard_map.46 = bf16[6,100,800]{2,1,0:T(8,128)(2,1)} custom-call(bf16[1632,512]{1,0:T(8,128)(2,1)} %fusion.6.fin, bf16[8,6,112,128]{3,2,1,0:T(8,128)(2,1)} %pad.9.hin), custom_call_target="tpu_custom_call" | custom-call | tf_op jit(solution)/shard_map/pallas_call | solution.py:246
  112.8 2.3 %copy.7 = bf16[6,100,800]{2,1,0:T(8,128)(2,1)} copy(bf16[6,100,800]{2,1,0:T(8,128)(2,1)} %shard_map.46) | data formatting | bytes 1920000
Async XLA Ops:
  3.2 1.7 %copy-start.1 = (bf16[1000,800]{0,1:T(8,128)(2,1)S(1)}, bf16[1000,800]{0,1:T(8,128)(2,1)}, u32[]{:S(2)}) copy-start(bf16[1000,800]{0,1:T(8,128)(2,1)} %param.6) | copy-start | bytes 4800004
  3.5 2.2 %copy-start = (bf16[1000,800]{0,1:T(8,128)(2,1)S(1)}, bf16[1000,800]{0,1:T(8,128)(2,1)}, u32[]{:S(2)}) copy-start(bf16[1000,800]{0,1:T(8,128)(2,1)} %param.5) | copy-start | bytes 4800004
  3.6 2.2 %copy-start.2 = (bf16[1000,24]{0,1:T(8,128)(2,1)S(1)}, bf16[1000,24]{0,1:T(8,128)(2,1)}, u32[]{:S(2)}) copy-start(bf16[1000,24]{0,1:T(8,128)(2,1)} %param.7) | copy-start | bytes 144004

commit v4 on v3

--- a/solution.py
+++ b/solution.py
@@ -47,8 +47,9 @@
            fz_s, fz_r, fp_s, fp_r, fd_s, fd_r, h_s, h_r, y_s, y_r, a_s, a_r, r_s, r_r, loc):
     f32, bf16 = jnp.float32, jnp.bfloat16
     S, C = R // Z, R // 2
-    count, tall, lanes = X.shape[1:]
-    size = out.shape[1]
+    tall = X.shape[1]
+    count, size = out.shape[:2]
+    lanes = 128
     K = A.shape[2]
     r, z = lax.axis_index("row"), lax.axis_index("col")
     p, core = r // 2, lax.rem(r, 2)
@@ -75,14 +76,19 @@
     def lane(q):
         return pl.ds(pl.multiple_of(q * wide, 128), wide)
 
-    def along(side, step, src, src_ref):
-        return send(src_ref, F.at[src, :, lane(p)], fz_s.at[side, step - 1], fz_r.at[side, step - 1],
-                    r, z + 1 - 2 * side)
-
-    firsts = [along(side, 1, z, fin.at[:, lane(p)]) for side in range(2)]
+    cut = L // 32 * 16
+    parts = (pl.ds(0, cut), pl.ds(cut, L - cut))
+
+    def along(side, step, src, h, src_ref):
+        return send(src_ref, F.at[src, parts[h], lane(p)], fz_s.at[side, step - 1, h],
+                    fz_r.at[side, step - 1, h], r, z + 1 - 2 * side)
+
     can = [z + 1 < Z, z > 0]
-    for side in range(2):
-        pl.when(can[side])(firsts[side].start)
+    firsts = []
+    for h in range(2):
+        for side in range(2):
+            firsts.append((can[side], along(side, 1, z, h, fin.at[parts[h], lane(p)])))
+            pl.when(can[side])(firsts[-1][1].start)
     hs = []
     for d in range(1, Z):
         to = lax.rem(z + d, Z)
@@ -94,37 +100,39 @@
     near = jnp.minimum(z, Z - 1 - z)
     longer = jnp.where(z > Z - 1 - z, 0, 1)
     blocks = []
-    cut = L // 32 * 16
     for k in range(1, Z):
         paired = k <= 2 * near
         step = jnp.where(paired, (k + 1) // 2, k - near)
         side = jnp.where(paired, (k - 1) % 2, longer)
         src = z + step * (2 * side - 1)
-        come = along(side, step, src, F.at[src, :, lane(p)])
-        go = along(side, step + 1, src, F.at[src, :, lane(p)])
         on = jnp.where(side == 0, z + 1 < Z, z > 0)
-        mine = F.at[src, :, lane(p)]
-        plane = [send(mine, mine, fp_s.at[k - 1, g], fp_r.at[k - 1, g], to * 2 + core, z)
-                 for g, to in enumerate((px, py))]
-        high = F.at[src, pl.ds(0, cut), lane(px)]
-        low = F.at[src, pl.ds(cut, L - cut), lane(py)]
+        come, go, plane = [], [], []
+        for h in range(2):
+            mine = F.at[src, parts[h], lane(p)]
+            come.append(along(side, step, src, h, mine))
+            go.append(along(side, step + 1, src, h, mine))
+            plane.append([send(mine, mine, fp_s.at[k - 1, h, g], fp_r.at[k - 1, h, g], to * 2 + core, z)
+                          for g, to in enumerate((px, py))])
+        high = F.at[src, parts[0], lane(px)]
+        low = F.at[src, parts[1], lane(py)]
         corner = [send(high, high, fd_s.at[k - 1, 0], fd_r.at[k - 1, 0], py * 2 + core, z),
                   send(low, low, fd_s.at[k - 1, 1], fd_r.at[k - 1, 1], px * 2 + core, z)]
         blocks.append((src, come, go, on, plane, corner))
-        sent += plane + corner
+        sent += plane[0] + plane[1] + corner
 
     def arrive(k):
         src, come, go, on, plane, corner = blocks[k - 1]
-        come.wait_recv()
-        pl.when(on)(go.start)
-        for c in plane:
-            c.start()
+        for h in range(2):
+            come[h].wait_recv()
+            pl.when(on)(go[h].start)
+            plane[h][h].start()
+            plane[h][1 - h].start()
 
     def turn(k):
         plane, corner = blocks[k - 1][4:]
-        for c, f in zip(plane, corner):
-            c.wait_recv()
-            f.start()
+        for h in range(2):
+            plane[h][h].wait_recv()
+            corner[h].start()
 
     arrive(1)
     for k in range(2, Z - 1):
@@ -149,21 +157,31 @@
         c.wait_recv()
     mine.wait()
 
-    @pl.loop(0, count)
-    def _(i):
+    at = lax.broadcasted_iota(jnp.int32, (tall, lanes), 1)
+
+    def take(ref, j, i):
+        q, rem = divmod(i * size, lanes)
+        v = ref[j, :, q * lanes:(q + 1) * lanes].astype(f32)
+        if rem:
+            v = pltpu.roll(v, lanes - rem, 1)
+        if rem + size > lanes:
+            more = ref[j, :, (q + 1) * lanes:(q + 2) * lanes].astype(f32)
+            v = jnp.where(at < lanes - rem, v, pltpu.roll(more, lanes - rem, 1))
+        return jnp.where(at < size, v, 0.0)
+
+    for i in range(count):
         tiles = [jnp.zeros((tall, lanes), f32) for _ in range(K // 128)]
         for j in range(R):
-            y = jnp.concatenate([Y[j, i].astype(f32), jnp.zeros((lanes - tall, lanes), f32)], axis=0)
-            v = X[j, i].astype(f32) - jnp.transpose(y)[:tall]
+            y = jnp.concatenate([take(Y, j, i), jnp.zeros((lanes - tall, lanes), f32)], axis=0)
+            v = take(X, j, i) - jnp.transpose(y)[:tall]
             q, rem = divmod(j * size, 128)
             if rem + size <= 128:
                 tiles[q] += pltpu.roll(v, rem, 1) if rem else v
             else:
                 w = pltpu.roll(v, rem, 1)
-                at = lax.broadcasted_iota(jnp.int32, (tall, lanes), 1)
                 tiles[q] += jnp.where(at >= rem, w, 0.0)
                 tiles[q + 1] += jnp.where(at < rem, w, 0.0)
-        start = pl.multiple_of(i * tall, 16)
+        start = i * tall
         for q in range(K // 128):
             A[0, pl.ds(start, tall), pl.ds(q * 128, 128)] = tiles[q].astype(bf16)
 
@@ -192,7 +210,7 @@
     sent.append(back)
     for k in range(Z):
         if k:
-            for c in blocks[k - 1][5]:
+            for c in blocks[k - 1][5] + [blocks[k - 1][4][0][1], blocks[k - 1][4][1][0]]:
                 c.wait_recv()
             block = F.at[blocks[k - 1][0]]
         else:
@@ -218,10 +236,11 @@
         out[i] = (acc[0, rows, :] + rr[rows, :].astype(f32)).astype(bf16)[: out.shape[1]]
     for c in sent:
         c.wait_send()
-    for side in range(2):
-        pl.when(can[side])(firsts[side].wait_send)
+    for there, c in firsts:
+        pl.when(there)(c.wait_send)
     for block in blocks:
-        pl.when(block[3])(block[2].wait_send)
+        for c in block[2]:
+            pl.when(block[3])(c.wait_send)
 
 
 def fused(R, Z, halves, first_factor, second_factor, weights):
@@ -231,7 +250,7 @@
     q, v = first_factor.shape
     n = second_factor.shape[1]
     count, step = O // Z, b // S
-    tall, lanes = up(a, 16), 128
+    tall = up(a, 16)
     K = up(R * a, 128)
     wide = up(-(-q // R), 128)
     core = lax.rem(lax.axis_index("row"), 2)
@@ -239,8 +258,9 @@
     full = jnp.concatenate([first_factor.T, second_factor.T, weights.T], axis=0)
     full = jnp.pad(full, ((0, L - R * a - n - O), (0, R * wide - q)))
     fin = lax.dynamic_slice_in_dim(full, core * (C * wide), C * wide, 1)
-    hin = halves.reshape(Z, count, a, S, step).transpose(0, 3, 1, 2, 4).reshape(R, count, a, step)
-    hin = jnp.pad(hin, ((0, 0), (0, 0), (0, tall - a), (0, lanes - step)))
+    hin = halves.reshape(Z, count, a, S, step).transpose(0, 3, 2, 1, 4).reshape(R, a, count * step)
+    lanes = up(count * step, 128)
+    hin = jnp.pad(hin, ((0, 0), (0, tall - a), (0, lanes - count * step)))
     dma, vmem = pltpu.SemaphoreType.DMA, pltpu.VMEM
     big = pl.BlockSpec(memory_space=pltpu.VMEM)
     return pl.pallas_call(
@@ -250,15 +270,15 @@
         out_specs=big,
         scratch_shapes=[
             vmem((Z, L, C * wide), bf16),
-            vmem((R, count, tall, lanes), bf16),
-            vmem((R, count, tall, lanes), bf16),
+            vmem((R, tall, lanes), bf16),
+            vmem((R, tall, lanes), bf16),
             vmem((2, count * tall, K), bf16),
             vmem((2, count * tall, n), jnp.float32),
             vmem((up(count, 16), C * wide), jnp.float32),
             vmem((count * tall, n), bf16),
             vmem((count * tall, n), bf16),
-            dma((2, Z)), dma((2, Z)),
-            dma((Z - 1, 2)), dma((Z - 1, 2)),
+            dma((2, Z, 2)), dma((2, Z, 2)),
+            dma((Z - 1, 2, 2)), dma((Z - 1, 2, 2)),
             dma((Z - 1, 2)), dma((Z - 1, 2)),
             dma((Z - 1,)), dma((Z - 1,)),
             dma((R - 1,)), dma((R - 1,)),

time: 115 us -> 110 us (0.957)
  Pallas kernels: 105 us -> 95.2 us
  local copies, waits for them, and re-layouts: 8 us -> 11.2 us
    pallas_call x1, Pallas kernels: 105 us -> 95.2 us  [fused(): pl.pallas_call(functools.partial(kernel, R, Z, n, wide, L), out_shape=jax...]
    reshape x2 -> x3, local copies, waits for them, and re-layouts: 3.52 us -> 7.07 us  [fused(): halves.reshape(Z, count, a, S, step).transpose(0, 3, 2, 1, 4)]
    unnamed x7 -> x5, local copies, waits for them, and re-layouts: 3.13 us -> 3.05 us
where the time goes in v4:
time: 110 us
  Pallas kernels  95.2 us (87%)
  local copies, waits for them, and re-layouts  11.2 us (10%)
  other arithmetic  3.14 us (3%)
    pallas_call x1, Pallas kernels, fused(): pl.pallas_call(functools.partial(kernel, R, Z, n, wide, L), out_shape=jax...  95.2 us
    reshape x3, local copies, waits for them, and re-layouts, fused(): halves.reshape(Z, count, a, S, step).transpose(0, 3, 2, 1, 4)  7.07 us
    concatenate x1, other arithmetic, fused(): full = jnp.concatenate([first_factor.T, second_factor.T, weights.T], axis=0)  3.14 us
    unnamed x5, local copies, waits for them, and re-layouts  3.05 us

profile of v4, /device:TPU:1, one launch (start us, length us, event | category | flops | bytes accessed | tf_op | source)
XLA Modules:
  0.0 109.6 jit_solution(697567420351335213)
XLA Ops:
  0.0 3.2 %reshape.6 = bf16[4,6,100,2,100]{4,3,1,0,2:T(2,128)(2,1)S(1)} reshape(bf16[24,100,200]{2,0,1:T(8,128)(2,1)} %param.4) | data formatting | bytes 1920000 | tf_op jit(solution)/shard_map/reshape | solution.py:261
  3.2 2.4 %copy.6 = bf16[4,6,100,2,100]{2,3,0,4,1:T(2,128)(2,1)S(1)} copy(bf16[4,6,100,2,100]{4,3,1,0,2:T(2,128)(2,1)S(1)} %reshape.6) | data formatting | bytes 1920000 | tf_op jit(solution)/shard_map/reshape | solution.py:261
  5.6 1.5 %copy.7 = bf16[8,100,600]{2,1,0:T(8,128)(2,1)S(1)} copy(bf16[8,100,600]{1,0,2:T(8,128)(2,1)S(1)} %bitcast.8) | data formatting | bytes 1920000 | tf_op jit(solution)/shard_map/reshape | solution.py:261
  7.1 0.0 copy-start
  7.1 0.0 copy-start.1
  7.1 1.1 %pad.9.hin = bf16[8,112,640]{2,1,0:T(8,128)(2,1)} pad(bf16[8,100,600]{2,1,0:T(8,128)(2,1)S(1)} %copy.7, bf16[]{:T(256)} %constant.5.clone.1), padding=0_0x0_12x0_40 | pad | bytes 2106882 | tf_op jit(solution)/shard_map/jit(_pad)/pad | solution.py:263
  8.2 0.7 copy-done
  8.9 0.0 copy-done.1
  8.9 3.1 %fusion.6.fin = bf16[1632,512]{1,0:T(8,128)(2,1)} fusion(s32[]{:T(128)S(6)} %select_n.3, bf16[800,1000]{1,0:T(8,128)(2,1)S(1)} %bitcast.9, bf16[800,1000]{1,0:T(8,128)(2,1)} %bitcast.10, bf16[24,1000]{1,0:T(8,128)(2,1)S(1)} %bitcast.11), kind=kLoop, calls=%fused_computation.11 | loop fusion | flops 13369344 | bytes 4920192 | tf_op jit(solution)/shard_map/concatenate | solution.py:258
  12.1 95.2 %shard_map.46 = bf16[6,100,800]{2,1,0:T(8,128)(2,1)} custom-call(bf16[1632,512]{1,0:T(8,128)(2,1)} %fusion.6.fin, bf16[8,112,640]{2,1,0:T(8,128)(2,1)} %pad.9.hin), custom_call_target="tpu_custom_call" | custom-call | tf_op jit(solution)/shard_map/pallas_call | solution.py:266
  107.3 2.3 %copy.9 = bf16[6,100,800]{2,1,0:T(8,128)(2,1)} copy(bf16[6,100,800]{2,1,0:T(8,128)(2,1)} %shard_map.46) | data formatting | bytes 1920000
Async XLA Ops:
  7.1 1.8 %copy-start = (bf16[1000,800]{0,1:T(8,128)(2,1)S(1)}, bf16[1000,800]{0,1:T(8,128)(2,1)}, u32[]{:S(2)}) copy-start(bf16[1000,800]{0,1:T(8,128)(2,1)} %param.5) | copy-start | bytes 4800004
  7.1 1.8 %copy-start.1 = (bf16[1000,24]{0,1:T(8,128)(2,1)S(1)}, bf16[1000,24]{0,1:T(8,128)(2,1)}, u32[]{:S(2)}) copy-start(bf16[1000,24]{0,1:T(8,128)(2,1)} %param.7) | copy-start | bytes 144004

commit v5 on v4

--- a/solution.py
+++ b/solution.py
@@ -135,9 +135,9 @@
             corner[h].start()
 
     arrive(1)
+    turn(1)
     for k in range(2, Z - 1):
         arrive(k)
-    turn(1)
     for c in hs:
         c.wait_recv()
     own.wait()

time: 110 us -> 105 us (0.955)
  Pallas kernels: 95.2 us -> 90.7 us
    pallas_call x1, Pallas kernels: 95.2 us -> 90.7 us  [fused(): pl.pallas_call(functools.partial(kernel, R, Z, n, wide, L), out_shape=jax...]
where the time goes in v5:
time: 105 us
  Pallas kernels  90.7 us (86%)
  local copies, waits for them, and re-layouts  11.2 us (11%)
  other arithmetic  3.14 us (3%)
    pallas_call x1, Pallas kernels, fused(): pl.pallas_call(functools.partial(kernel, R, Z, n, wide, L), out_shape=jax...  90.7 us
    reshape x3, local copies, waits for them, and re-layouts, fused(): halves.reshape(Z, count, a, S, step).transpose(0, 3, 2, 1, 4)  7.07 us
    concatenate x1, other arithmetic, fused(): full = jnp.concatenate([first_factor.T, second_factor.T, weights.T], axis=0)  3.14 us
    unnamed x5, local copies, waits for them, and re-layouts  3.05 us

profile of v5, /device:TPU:1, one launch (start us, length us, event | category | flops | bytes accessed | tf_op | source)
XLA Modules:
  0.0 105.2 jit_solution(4769397471093918933)
XLA Ops:
  0.0 3.2 %reshape.6 = bf16[4,6,100,2,100]{4,3,1,0,2:T(2,128)(2,1)S(1)} reshape(bf16[24,100,200]{2,0,1:T(8,128)(2,1)} %param.4) | data formatting | bytes 1920000 | tf_op jit(solution)/shard_map/reshape | solution.py:261
  3.2 2.4 %copy.6 = bf16[4,6,100,2,100]{2,3,0,4,1:T(2,128)(2,1)S(1)} copy(bf16[4,6,100,2,100]{4,3,1,0,2:T(2,128)(2,1)S(1)} %reshape.6) | data formatting | bytes 1920000 | tf_op jit(solution)/shard_map/reshape | solution.py:261
  5.6 1.5 %copy.7 = bf16[8,100,600]{2,1,0:T(8,128)(2,1)S(1)} copy(bf16[8,100,600]{1,0,2:T(8,128)(2,1)S(1)} %bitcast.8) | data formatting | bytes 1920000 | tf_op jit(solution)/shard_map/reshape | solution.py:261
  7.1 0.0 copy-start
  7.1 0.0 copy-start.1
  7.1 1.1 %pad.9.hin = bf16[8,112,640]{2,1,0:T(8,128)(2,1)} pad(bf16[8,100,600]{2,1,0:T(8,128)(2,1)S(1)} %copy.7, bf16[]{:T(256)} %constant.5.clone.1), padding=0_0x0_12x0_40 | pad | bytes 2106882 | tf_op jit(solution)/shard_map/jit(_pad)/pad | solution.py:263
  8.2 0.7 copy-done
  8.9 0.0 copy-done.1
  8.9 3.1 %fusion.6.fin = bf16[1632,512]{1,0:T(8,128)(2,1)} fusion(s32[]{:T(128)S(6)} %select_n.3, bf16[800,1000]{1,0:T(8,128)(2,1)S(1)} %bitcast.9, bf16[800,1000]{1,0:T(8,128)(2,1)} %bitcast.10, bf16[24,1000]{1,0:T(8,128)(2,1)S(1)} %bitcast.11), kind=kLoop, calls=%fused_computation.11 | loop fusion | flops 13369344 | bytes 4920192 | tf_op jit(solution)/shard_map/concatenate | solution.py:258
  12.1 90.7 %shard_map.46 = bf16[6,100,800]{2,1,0:T(8,128)(2,1)} custom-call(bf16[1632,512]{1,0:T(8,128)(2,1)} %fusion.6.fin, bf16[8,112,640]{2,1,0:T(8,128)(2,1)} %pad.9.hin), custom_call_target="tpu_custom_call" | custom-call | tf_op jit(solution)/shard_map/pallas_call | solution.py:266
  102.8 2.3 %copy.9 = bf16[6,100,800]{2,1,0:T(8,128)(2,1)} copy(bf16[6,100,800]{2,1,0:T(8,128)(2,1)} %shard_map.46) | data formatting | bytes 1920000
Async XLA Ops:
  7.1 1.8 %copy-start = (bf16[1000,800]{0,1:T(8,128)(2,1)S(1)}, bf16[1000,800]{0,1:T(8,128)(2,1)}, u32[]{:S(2)}) copy-start(bf16[1000,800]{0,1:T(8,128)(2,1)} %param.5) | copy-start | bytes 4800004
  7.1 1.8 %copy-start.1 = (bf16[1000,24]{0,1:T(8,128)(2,1)S(1)}, bf16[1000,24]{0,1:T(8,128)(2,1)}, u32[]{:S(2)}) copy-start(bf16[1000,24]{0,1:T(8,128)(2,1)} %param.7) | copy-start | bytes 144004
